TPU v7x, 1024 devices: a whole 8x8x8 slice. The times are simulated.
1024 devices in a mesh: expert: 64 (over y, x), tensor: 16 (over z, core).
Axes of the slice: x: 8, y: 8, z: 8, core: 2. Of those that a mesh axis runs over, the one named last changes fastest.
Arguments:
- tokens: bfloat16 [8192, 2048], P('expert', 'tensor')
- norm_gain: float32 [2048], replicated, may hold values from 0.5 to 1.5
- picks: int32 [32, 512], replicated, may hold values from 0 to 8191, as said below
- gates: float32 [32, 512], replicated, may hold values from 0.1 to 1
- shared_gate: bfloat16 [2048, 2048], P(None, 'tensor'), may hold values from -0.125 to 0.125
- shared_up: bfloat16 [2048, 2048], P(None, 'tensor'), may hold values from -0.125 to 0.125
- shared_down: bfloat16 [2048, 2048], P('tensor'), may hold values from -0.125 to 0.125
- expert_in: bfloat16 [64, 2048, 4096], P('expert', None, 'tensor'), may hold values from -0.125 to 0.125
- expert_out: bfloat16 [64, 4096, 2048], P('expert', 'tensor'), may hold values from -0.0625 to 0.0625
Outputs:
- mixed: bfloat16 [8192, 2048], P('expert', 'tensor')
Inputs may be any that keep to these rules, and one draw needn't show every extreme that they name: Each expert's list names 512 different tokens. Calling tokens 128 * s to 128 * s + 127 group s, at most 16 of one expert's picks lie in one group, and every expert's list has exactly 16 in some group.
All inputs are finite; a program needn't handle non-finite values.
Results may differ from a plain program's by a relative error of at most 0.024.
Values may be sent and summed in bfloat16 or wider, within the bound.
A program may use at most 32 MiB of HBM per device.

v0:
```python
import jax
import jax.numpy as jnp
from jax import lax
from jax.sharding import PartitionSpec as P

EPS = 1e-06


def absorb_rows(piece, gain_all, matrices):
    widened = piece.astype(jnp.float32)
    scaled = (widened * gain_all).astype(jnp.bfloat16)
    updated = [jnp.dot(scaled, matrix, preferred_element_type=jnp.float32) for matrix in matrices]
    return tuple(updated) + (jnp.sum(widened * widened, axis=1),)


def project_rows(weights, hidden):
    return lax.dot_general(
        weights, hidden, (((0,), (1,)), ((), ())), preferred_element_type=jnp.float32
    )


def shards(
    tokens, norm_gain, picks, gates, shared_gate, shared_up, shared_down, expert_in, expert_out
):
    holders = lax.axis_size("expert")
    holder = lax.axis_index("expert")
    group_rows, slice_width = tokens.shape
    expert_count, capacity = picks.shape
    slot_bound = 2 * capacity // holders
    slot_total = holders * slot_bound
    model_width = norm_gain.shape[0]
    sources = picks // group_rows
    local_rows = picks - sources * group_rows
    is_mine = sources == holder
    triangle = (
        lax.broadcasted_iota(jnp.int32, (capacity, capacity), 0)
        <= lax.broadcasted_iota(jnp.int32, (capacity, capacity), 1)
    ).astype(jnp.bfloat16)
    ranking = (
        jnp.dot(is_mine.astype(jnp.bfloat16), triangle, preferred_element_type=jnp.float32).astype(
            jnp.int32
        )
        - 1
    )
    slot_ids = lax.broadcasted_iota(jnp.int32, (1, slot_bound, 1), 1)
    matching = is_mine[:, None, :] & (ranking[:, None, :] == slot_ids)
    found = jnp.any(matching, axis=2)
    chosen_rows = jnp.sum(jnp.where(matching, local_rows[:, None, :], 0), axis=2)
    send_rows = jnp.where(found, chosen_rows, group_rows).reshape(-1)
    sender = (send_rows[:, None] == lax.broadcasted_iota(jnp.int32, (1, group_rows), 1)).astype(
        jnp.bfloat16
    )
    outgoing = jnp.dot(sender, tokens, preferred_element_type=jnp.float32).astype(jnp.bfloat16)
    outgoing = jnp.repeat(outgoing.reshape(expert_count, slot_bound, slice_width), 2, axis=0)
    arrived = lax.all_to_all(outgoing, "expert", split_axis=0, concat_axis=0, tiled=True)
    my_expert = holder // 2
    chosen = lax.dynamic_index_in_dim(picks, my_expert, 0, keepdims=False)
    gate_row = lax.dynamic_index_in_dim(gates, my_expert, 0, keepdims=False)
    anchors = chosen // group_rows
    positions = lax.broadcasted_iota(jnp.int32, (capacity, capacity), 0)
    earlier = lax.broadcasted_iota(jnp.int32, (capacity, capacity), 1)
    same_anchor = (anchors[:, None] == anchors[None, :]) & (earlier < positions)
    order_in_anchor = jnp.sum(same_anchor.astype(jnp.int32), axis=1)
    slot_index = anchors * slot_bound + order_in_anchor
    picker = (slot_index[:, None] == lax.broadcasted_iota(jnp.int32, (1, slot_total), 1)).astype(
        jnp.bfloat16
    )
    compact = jnp.dot(
        picker, arrived.reshape(slot_total, slice_width), preferred_element_type=jnp.float32
    ).astype(jnp.bfloat16)
    own_part = absorb_rows(
        lax.all_gather(tokens, "tensor", axis=1, tiled=True), norm_gain, (shared_gate, shared_up)
    )
    picked_part = absorb_rows(
        lax.all_gather(compact, "tensor", axis=1, tiled=True), norm_gain, (expert_in[0],)
    )
    own_scale = lax.rsqrt(own_part[2] / model_width + EPS)[:, None]
    shared_hidden = (jax.nn.silu(own_scale * own_part[0]) * (own_scale * own_part[1])).astype(
        jnp.bfloat16
    )
    picked_scale = lax.rsqrt(picked_part[1] / model_width + EPS)[:, None]
    activation = jax.nn.gelu(picked_scale * picked_part[0], approximate=False).astype(jnp.bfloat16)
    joined = lax.psum_scatter(
        jnp.concatenate(
            [project_rows(expert_out[0], activation), project_rows(shared_down, shared_hidden)],
            axis=1,
        ).astype(jnp.bfloat16),
        "tensor",
        scatter_dimension=0,
        tiled=True,
    ).astype(jnp.float32)
    expert_part = joined[:, :capacity].T
    shared_part = joined[:, capacity:].T
    gated = (gate_row[:, None] * expert_part).astype(jnp.bfloat16)
    returning = lax.dot_general(
        picker, gated, (((0,), (0,)), ((), ())), preferred_element_type=jnp.float32
    ).astype(jnp.bfloat16)
    returned = lax.all_to_all(
        returning.reshape(holders, slot_bound, slice_width),
        "expert",
        split_axis=0,
        concat_axis=0,
        tiled=True,
    )
    return_rows = jnp.repeat(send_rows.reshape(expert_count, slot_bound), 2, axis=0).reshape(-1)
    selector = (
        lax.broadcasted_iota(jnp.int32, (group_rows, slot_total), 0) == return_rows[None, :]
    ).astype(jnp.bfloat16)
    mixture = jnp.dot(
        selector, returned.reshape(slot_total, slice_width), preferred_element_type=jnp.float32
    )
    return (shared_part + mixture).astype(jnp.bfloat16)


def solution(mesh):
    placed = (
        P("expert", "tensor"),
        P(),
        P(),
        P(),
        P(None, "tensor"),
        P(None, "tensor"),
        P("tensor", None),
        P("expert", None, "tensor"),
        P("expert", "tensor", None),
    )
    return jax.shard_map(
        shards, mesh=mesh, in_specs=placed, out_specs=P("expert", "tensor"), check_vma=False
    )
```

profile of v0, /device:TPU:2, one launch (start us, length us, event | category | flops | bytes accessed | tf_op | source)
XLA Modules:
  0.0 210.0 jit_solution(4667272323552109893)
XLA Ops:
  6.5 0.0 copy-start
  6.5 0.0 copy-start.3
  6.5 0.0 copy-start.4
  6.5 1.0 multiply_subtract_fusion
  7.5 0.9 fusion.91
  8.4 0.0 copy-start.1
  8.4 0.0 copy-start.2
  8.4 0.2 fusion.15
  8.6 0.6 fusion.26
  9.3 0.6 select_reduce_fusion
  9.9 0.1 select_n.53
  10.0 1.0 convolution_convert_fusion.2
  11.0 0.7 broadcast_in_dim.36
  11.8 17.2 %all-to-all-start = ((bf16[64,16,128]{2,1,0:T(8,128)(2,1)}), bf16[64,16,128]{2,1,0:T(8,128)(2,1)S(1)}, u32[]{:S(2)}, u32[]{:S(2)}) async-start(bf16[64,16,128]{2,1,0:T(8,128)(2,1)} %bitcast.3), calls=%async_computation | async-start | bytes 524288 | tf_op jit(solution)/shard_map/all_to_all | solution.py:55
  29.0 0.0 all-gather.2.cloned.1.call-start
  29.1 0.7 and_select_fusion
  29.8 0.2 convert_reduce_fusion
  30.1 12.0 %all-to-all-done = bf16[64,16,128]{2,1,0:T(8,128)(2,1)S(1)} async-done(((bf16[64,16,128]{2,1,0:T(8,128)(2,1)}), bf16[64,16,128]{2,1,0:T(8,128)(2,1)S(1)}, u32[]{:S(2)}, u32[]{:S(2)}) %all-to-all-start) | async-done | bytes 262176 | tf_op jit(solution)/shard_map/all_to_all | solution.py:55
  42.1 1.2 fusion.13
  43.3 0.0 all-gather.2.cloned.1.call-update
  43.3 0.0 reduce-scatter.4.cloned.1.call-start
  43.4 0.0 copy-done.3
  43.4 28.8 %all_gather.7 = bf16[128,2048]{1,0:T(8,128)(2,1)S(1)} all-gather(bf16[128,128]{1,0:T(8,128)(2,1)S(1)} %copy-done.3), channel_id=1, replica_groups=mesh['expert'=64,'tensor'=16] {'tensor'}, dimensions={1}, use_global_device_ids=true | all-gather | bytes 557056 | tf_op jit(solution)/shard_map/all_gather | solution.py:72
  72.1 0.2 fusion.18
  72.3 0.0 copy-done.4
  72.3 1.3 convolution_multiply_fusion.1
  73.7 0.0 copy-done.1
  73.7 0.0 copy-done.2
  73.7 0.5 fusion.3
  74.2 17.9 %all-gather.2.cloned.1.call-done = bf16[512,2048]{1,0:T(8,128)(2,1)} async-done(((bf16[512,128]{1,0:T(8,128)(2,1)}), bf16[512,2048]{1,0:T(8,128)(2,1)}) %all-gather.2.cloned.1.call-update) | async-done | bytes 2097168 | tf_op jit(solution)/shard_map/all_gather | solution.py:75
  92.2 2.1 fusion
  94.3 0.0 copy-done
  94.3 6.5 %fusion.2 = bf16[2048,512]{0,1:T(8,128)(2,1)} fusion(bf16[1,256,2048]{2,1,0:T(8,128)(2,1)S(1)} %copy-done, bf16[1,2048,256]{2,1,0:T(8,128)(2,1)} %param.16, bf16[512,2048]{1,0:T(8,128)(2,1)} %all-gather.2.cloned.1.call-done, f32[2048]{0:T(1024)S(1)} %copy-done.4, f32[512]{0:T(512)S(1)} %add_rsqrt_fusion), kind=kOutput, calls=%fused_computation.5 | convolution fusion | flops 1086586880 | bytes 6301696 | tf_op jit(solution)/shard_map/dot_general | solution.py:17
  100.8 3.4 %pad_maximum_fusion = bf16[2048,640]{0,1:T(8,128)(2,1)} fusion(bf16[2048,128]{0,1:T(8,128)(2,1)S(1)} %fusion.3, bf16[2048,512]{0,1:T(8,128)(2,1)} %fusion.2), kind=kLoop, calls=%fused_computation.6 | loop fusion | flops 5242880 | bytes 5242880 | tf_op jit(solution)/shard_map/concatenate | solution.py:84
  104.2 4.4 %copy.10 = bf16[2048,640]{1,0:T(8,128)(2,1)} copy(bf16[2048,640]{0,1:T(8,128)(2,1)} %pad_maximum_fusion) | data formatting | bytes 5242880
  108.6 0.0 reduce-scatter.4.cloned.1.call-update
  108.7 0.7 constant_dynamic-slice_fusion
  109.4 64.4 %reduce-scatter.4.cloned.1.call-done = bf16[128,640]{1,0:T(8,128)(2,1)} async-done(((bf16[2048,640]{1,0:T(8,128)(2,1)}), bf16[128,640]{1,0:T(8,128)(2,1)}) %reduce-scatter.4.cloned.1.call-update) | async-done | bytes 163856
  173.8 1.1 copy.11
  174.9 1.6 fusion.12
  176.5 12.8 %all-to-all-start.1 = ((bf16[64,16,128]{2,1,0:T(8,128)(2,1)}), bf16[64,16,128]{2,1,0:T(8,128)(2,1)S(1)}, u32[]{:S(2)}, u32[]{:S(2)}) async-start(bf16[64,16,128]{2,1,0:T(8,128)(2,1)} %bitcast.11), calls=%async_computation.1 | async-start | bytes 524288 | tf_op jit(solution)/shard_map/all_to_all | solution.py:98
  189.3 0.1 eq.85
  189.4 12.9 %all-to-all-done.1 = bf16[64,16,128]{2,1,0:T(8,128)(2,1)S(1)} async-done(((bf16[64,16,128]{2,1,0:T(8,128)(2,1)}), bf16[64,16,128]{2,1,0:T(8,128)(2,1)S(1)}, u32[]{:S(2)}, u32[]{:S(2)}) %all-to-all-start.1) | async-done | bytes 262176 | tf_op jit(solution)/shard_map/all_to_all | solution.py:98
  202.4 0.8 fusion.17
  (7 shorter events, 0.1 us)
Async XLA Ops:
  6.5 87.7 %copy-start = (bf16[1,256,2048]{2,1,0:T(8,128)(2,1)S(1)}, bf16[1,256,2048]{2,1,0:T(8,128)(2,1)}, u32[]{:S(2)}) copy-start(bf16[1,256,2048]{2,1,0:T(8,128)(2,1)} %param.17) | copy-start | bytes 3145732
  6.5 36.8 %copy-start.3 = (bf16[128,128]{1,0:T(8,128)(2,1)S(1)}, bf16[128,128]{1,0:T(8,128)(2,1)}, u32[]{:S(2)}) copy-start(bf16[128,128]{1,0:T(8,128)(2,1)} %param.9) | copy-start | bytes 98308
  6.5 65.8 %copy-start.4 = (f32[2048]{0:T(1024)S(1)}, f32[2048]{0:T(1024)}, u32[]{:S(2)}) copy-start(f32[2048]{0:T(1024)} %param.10) | copy-start | bytes 24580
  8.4 65.3 %copy-start.1 = (bf16[128,2048]{1,0:T(8,128)(2,1)S(1)}, bf16[128,2048]{1,0:T(8,128)(2,1)}, u32[]{:S(2)}) copy-start(bf16[128,2048]{1,0:T(8,128)(2,1)} %param.15) | copy-start | bytes 1572868
  8.4 65.3 %copy-start.2 = (bf16[2048,128]{1,0:T(8,128)(2,1)S(1)}, bf16[2048,128]{1,0:T(8,128)(2,1)}, u32[]{:S(2)}) copy-start(bf16[2048,128]{1,0:T(8,128)(2,1)} %param.14) | copy-start | bytes 1572868
  11.8 30.4 %all-to-all-start = ((bf16[64,16,128]{2,1,0:T(8,128)(2,1)}), bf16[64,16,128]{2,1,0:T(8,128)(2,1)S(1)}, u32[]{:S(2)}, u32[]{:S(2)}) async-start(bf16[64,16,128]{2,1,0:T(8,128)(2,1)} %bitcast.3), calls=%async_computation | async-start | bytes 524288 | tf_op jit(solution)/shard_map/all_to_all | solution.py:55
  29.0 63.2 %all-gather.2.cloned.1.call-start = ((), (), s32[]{:S(2)}) async-start(), calls=%async_computation.3 | async-start | bytes 2228224 | tf_op jit(solution)/shard_map/all_gather | solution.py:75
  43.3 130.5 %reduce-scatter.4.cloned.1.call-start = ((), (), s32[]{:S(2)}) async-start(), calls=%async_computation.4 | async-start | bytes 2785280
  176.5 25.8 %all-to-all-start.1 = ((bf16[64,16,128]{2,1,0:T(8,128)(2,1)}), bf16[64,16,128]{2,1,0:T(8,128)(2,1)S(1)}, u32[]{:S(2)}, u32[]{:S(2)}) async-start(bf16[64,16,128]{2,1,0:T(8,128)(2,1)} %bitcast.11), calls=%async_computation.1 | async-start | bytes 524288 | tf_op jit(solution)/shard_map/all_to_all | solution.py:98
Sparse Core Ops, SparseCore 0:
  43.4 48.6 all-gather.1
  108.8 64.9 reduce-scatter.3
where the time goes:
time: 211 us; the launch traced here: 210 us
  waiting for transfers between devices  107 us (51%)
  starting transfers between devices  30.1 us (14%)
  blocking collectives  28.8 us (14%)
  between operations  13.6 us (6%)
  matrix products  13.2 us (6%)
  other arithmetic  9.87 us (5%)
  local copies, waits for them, and re-layouts  7.15 us (3%)
    unnamed x3, waiting for transfers between devices  64.5 us
    all_gather x1, blocking collectives, shards(): lax.all_gather(tokens, 'tensor', axis=1, tiled=True)  28.8 us
    all_gather x1, waiting for transfers between devices, shards(): lax.all_gather(compact, 'tensor', axis=1, tiled=True)  17.9 us
    all_to_all x1, starting transfers between devices, shards(): lax.all_to_all(outgoing, 'expert', split_axis=0, concat_axis=0, tiled=True)  17.2 us
    all_to_all x1, waiting for transfers between devices, shards(): lax.all_to_all(returning.reshape(holders, slot_bound, slice_width), 'expe...  12.9 us
    all_to_all x1, starting transfers between devices, shards(): lax.all_to_all(returning.reshape(holders, slot_bound, slice_width), 'expe...  12.8 us
    all_to_all x1, waiting for transfers between devices, shards(): lax.all_to_all(outgoing, 'expert', split_axis=0, concat_axis=0, tiled=True)  12 us
    dot_general x2, matrix products, project_rows(): lax.dot_general(weights, hidden, (((0,), (1,)), ((), ())), preferred_elem...  7.08 us
  transfers between devices with their start and end apart: 4, of which 4 were waited for; matrix products, arithmetic and copies ran while one was open for 2% of the time, Pallas kernels for 0%

commit v1 on v0

v1 whole, which is shorter than its diff:
```python
import jax
import jax.numpy as jnp
from jax import lax
from jax.experimental import pallas as pl
from jax.experimental.pallas import tpu as pltpu
from jax.sharding import PartitionSpec as P

EPS = 1e-06
BF = jnp.bfloat16
F32 = jnp.float32
MESH = pl.DeviceIdType.MESH
FAR_FIRST = (4, 3, 5, 2, 6, 1, 7)
ROOT_HALF = 0.7071067811865476


def one_hot(condition):
    return jnp.where(condition, 1.0, 0.0).astype(BF)


def dot(a, b):
    return jnp.dot(a, b, preferred_element_type=F32)


def wait_bytes(ref, sem):
    pltpu.make_async_copy(ref, ref, sem).wait()


def layer(
    tokens_hbm, gain_hbm, picks_hbm, gates_hbm, gate_hbm, up_hbm, down_hbm, in_hbm, out_hbm,
    result,
    tokens, gain, picks, gates, w_gate_up, w_down, w_in, w_out,
    selector, outgoing, mid, slots, picker, picker_t, gate_wide,
    own_tokens, shared_part, shared_sib, shared_send, shared_recv,
    gathered, hidden, squares, activation, partial, partial_sib, ring_send, ring_recv,
    expanded, ret_x, ret_mid, ret_y,
    load_sem, a2a_send, a2a_recv, tok_send, tok_recv, sib_send, sib_recv,
    ag_send, ag_recv, agsib_send, agsib_recv, rs_send, rs_recv, rssib_send, rssib_recv,
):
    e = lax.axis_index("expert")
    t = lax.axis_index("tensor")
    y, x = e // 8, e % 8
    z, c = t // 2, t % 2
    other = 1 - c
    half_rows = 256

    def at_y(k):
        return (((y + k) % 8) * 8 + x, t)

    def at_x(k):
        return (y * 8 + (x + k) % 8, t)

    def at_z(k):
        return (e, ((z + k) % 8) * 2 + c)

    sibling = (e, z * 2 + other)

    def remote(src, dst, send, recv, device):
        copy = pltpu.make_async_remote_copy(
            src, dst, send, recv, device_id=device, device_id_type=MESH
        )
        copy.start()
        return copy

    loads = [
        pltpu.make_async_copy(src, dst, load_sem.at[n])
        for n, (src, dst) in enumerate(
            [
                (picks_hbm, picks),
                (tokens_hbm, tokens),
                (gain_hbm, gain),
                (gates_hbm, gates),
                (gate_hbm, w_gate_up.at[:, pl.ds(0, 128)]),
                (up_hbm, w_gate_up.at[:, pl.ds(128, 128)]),
                (down_hbm, w_down),
                (in_hbm.at[0], w_in),
                (out_hbm.at[0], w_out),
            ]
        )
    ]
    for load in loads:
        load.start()

    barrier = pltpu.get_barrier_semaphore()
    for k in range(1, 8):
        for device in (at_y(k), at_x(k), at_z(k)):
            pl.semaphore_signal(barrier, inc=1, device_id=device, device_id_type=MESH)
    pl.semaphore_signal(barrier, inc=1, device_id=sibling, device_id_type=MESH)

    triangle = one_hot(
        lax.broadcasted_iota(jnp.int32, (512, 512), 0)
        <= lax.broadcasted_iota(jnp.int32, (512, 512), 1)
    )
    loads[0].wait()
    all_picks = picks[...]
    mine = (all_picks >> 7) == e
    rank = dot(one_hot(mine), triangle)
    rank = jnp.where(mine, rank, 0.0)
    local = (all_picks & 127).astype(F32) + 1.0
    slot_number = lax.broadcasted_iota(jnp.int32, (16, 512), 0).astype(F32) + 1.0
    row_number = lax.broadcasted_iota(jnp.int32, (16, 128), 1).astype(F32) + 1.0
    for n in range(32):
        matched = jnp.where(rank[n : n + 1, :] == slot_number, local[n : n + 1, :], 0.0)
        row = jnp.sum(matched, axis=1, keepdims=True)
        selector[n * 16 : (n + 1) * 16, :] = one_hot(row == row_number)
    loads[1].wait()
    out_rows = dot(selector[...], tokens[...]).astype(BF)
    outgoing[...] = out_rows.reshape(8, 64, 128)
    own_tokens[c, z] = tokens[...]
    mid[y] = outgoing[y]

    pl.semaphore_wait(barrier, 22)

    waits_send = []
    for k in FAR_FIRST:
        waits_send.append(
            remote(outgoing.at[(y + k) % 8], mid.at[y], a2a_send.at[0], a2a_recv.at[0], at_y(k))
        )
    tok_copies = [
        remote(own_tokens.at[c, z], own_tokens.at[c, z], tok_send.at[0], tok_recv.at[0], at_z(k))
        for k in FAR_FIRST
    ]

    chosen = picks[pl.ds(e // 2, 1), :]
    anchor = chosen >> 7
    from_group = anchor == lax.broadcasted_iota(jnp.int32, (64, 512), 0)
    counts = dot(one_hot(from_group), triangle)
    order = jnp.sum(jnp.where(from_group, counts, 0.0), axis=0, keepdims=True) - 1.0
    slot = (((anchor & 7) * 8 + (anchor >> 3)) * 16).astype(F32) + order

    wait_bytes(mid.at[pl.ds(0, 7)], a2a_recv.at[0])
    for k in FAR_FIRST:
        waits_send.append(
            remote(
                mid.at[:, pl.ds(((x + k) % 8) // 2 * 16, 16), :],
                slots.at[x],
                a2a_send.at[1],
                a2a_recv.at[1],
                at_x(k),
            )
        )
    slots[x] = mid[:, pl.ds(pl.multiple_of(x // 2 * 16, 16), 16), :]

    slot_wide = jnp.transpose(jnp.broadcast_to(slot, (128, 512)))
    lane = lax.broadcasted_iota(jnp.int32, (512, 128), 1).astype(F32)
    sublane = lax.broadcasted_iota(jnp.int32, (128, 512), 0).astype(F32)
    for b in range(8):
        picker[:, b * 128 : (b + 1) * 128] = one_hot(slot_wide == lane + b * 128.0)

    wait_bytes(own_tokens.at[0, pl.ds(0, 7)], tok_recv.at[0])
    tok_sib = remote(own_tokens.at[c], own_tokens.at[c], sib_send.at[0], sib_recv.at[0], sibling)

    def ag_copy(d, k, h):
        src = (z - k + 8) % 8 if d == 0 else (z + k) % 8
        ref = gathered.at[c, src, pl.ds(h * half_rows, half_rows)]
        return remote(ref, ref, ag_send.at[d, k, h], ag_recv.at[d, k, h], at_z(1 if d == 0 else 7))

    def ag_sib(src, h, n):
        ref = gathered.at[c, src, pl.ds(h * half_rows, half_rows)]
        return remote(ref, ref, agsib_send.at[n, h], agsib_recv.at[n, h], sibling)

    wait_bytes(slots.at[pl.ds(0, 7)], a2a_recv.at[1])
    ag_copies = []
    sib_copies = []
    for h in (0, 1):
        rows = pl.ds(h * half_rows, half_rows)
        gathered[c, z, rows] = dot(picker[rows, :], slots[...].reshape(1024, 128)).astype(BF)
        for d in (0, 1):
            ag_copies.append(ag_copy(d, 0, h))
        sib_copies.append(ag_sib(z, h, 0))

    for b in range(8):
        picker_t[b * 128 : (b + 1) * 128, :] = one_hot(slot == sublane + b * 128.0)
    loads[3].wait()
    gate_wide[...] = jnp.transpose(jnp.broadcast_to(gates[pl.ds(e // 2, 1), :], (128, 512)))
    loads[2].wait()

    def shared_branch():
        wait_bytes(own_tokens.at[other], sib_recv.at[0])
        for load in loads[4:7]:
            load.wait()
        scaled = []
        total = jnp.zeros((128, 128), F32)
        for n in range(16):
            wide = own_tokens[n % 2, n // 2].astype(F32)
            scaled.append((wide * gain[n : n + 1, :]).astype(BF))
            total = total + wide * wide
        inverse = lax.rsqrt(jnp.sum(total, axis=1, keepdims=True) / 2048.0 + EPS)
        both = inverse * dot(jnp.concatenate(scaled, axis=1), w_gate_up[...])
        gate_part = both[:, :128]
        shared_hidden = (gate_part / (1.0 + jnp.exp(-gate_part)) * both[:, 128:]).astype(BF)
        for n in range(16):
            term = dot(shared_hidden, w_down[:, n * 128 : (n + 1) * 128])
            shared_part[n % 2, n // 2] = term.astype(BF)
        return remote(
            shared_part.at[other], shared_sib, sib_send.at[1], sib_recv.at[1], sibling
        )

    def absorb(h, chunks, first=False):
        rows = pl.ds(h * half_rows, half_rows)
        scaled = []
        weights = []
        total = None
        for plane, src in chunks:
            feature = src * 2 + plane
            wide = gathered[plane, src, rows].astype(F32)
            scaled.append((wide * gain[pl.ds(feature, 1), :]).astype(BF))
            weights.append(w_in[pl.ds(pl.multiple_of(feature * 128, 128), 128), :])
            total = wide * wide if total is None else total + wide * wide
        product = dot(jnp.concatenate(scaled, axis=1), jnp.concatenate(weights, axis=0))
        if first:
            hidden[rows, :] = product
            squares[rows, :] = total
        else:
            hidden[rows, :] += product
            squares[rows, :] += total

    def sib_wait(src, h, n):
        wait_bytes(gathered.at[other, src, pl.ds(h * half_rows, half_rows)], agsib_recv.at[n, h])

    shared_copy = shared_branch()
    loads[7].wait()
    for h in (0, 1):
        sib_wait(z, h, 0)
        absorb(h, [(c, z), (other, z)], first=True)

    def ag_from(d, k):
        return (z + 7 - k) % 8 if d == 0 else (z + 1 + k) % 8

    previous = None
    for k in range(4):
        for hh in (0, 1):
            pair = [(0, hh), (1, 1 - hh)]
            if k == 3 and hh == 1:
                continue
            for d, h in pair:
                src = ag_from(d, k)
                wait_bytes(
                    gathered.at[c, src, pl.ds(h * half_rows, half_rows)], ag_recv.at[d, k, h]
                )
                if k < 2 or (k == 2 and hh == 0):
                    ag_copies.append(ag_copy(d, k + 1, h))
                sib_copies.append(ag_sib(src, h, 1 + k * 2 + d if k < 3 else 7))
        if previous is not None:
            for h in (0, 1):
                for d in (0, 1):
                    sib_wait(ag_from(d, previous), h, 1 + previous * 2 + d)
                absorb(h, [(p, ag_from(d, previous)) for d in (0, 1) for p in (c, other)])
        previous = k
    last = ag_from(0, 3)
    loads[8].wait()
    for h in (0, 1):
        rows = pl.ds(h * half_rows, half_rows)
        sib_wait(last, h, 7)
        absorb(h, [(c, last), (other, last)])
        inverse = lax.rsqrt(jnp.sum(squares[rows, :], axis=1, keepdims=True) / 2048.0 + EPS)
        value = inverse * hidden[rows, :]
        activation[rows, :] = (value * 0.5 * (1.0 + lax.erf(value * ROOT_HALF))).astype(BF)

    rs_copies = []

    def project(k):
        column = pl.multiple_of((z + k) % 8 * 256, 256)
        weight = w_out[:, pl.ds(column, 256)]
        for h in (0, 1):
            rows = pl.ds(h * half_rows, half_rows)
            term = dot(activation[rows, :], weight).astype(BF)
            partial[k, 0, rows] = term[:, :128]
            partial[k, 1, rows] = term[:, 128:]
        rs_copies.append(
            remote(
                partial.at[k, other], partial_sib.at[k], rssib_send.at[k], rssib_recv.at[k], sibling
            )
        )

    arrived = set()

    def chip_sum(k, h):
        if k not in arrived:
            arrived.add(k)
            wait_bytes(partial_sib.at[k], rssib_recv.at[k])
        rows = pl.ds(h * half_rows, half_rows)
        return partial[k, c, rows].astype(F32) + partial_sib[k, rows].astype(F32)

    def ring_in(d, k, h):
        wait_bytes(ring_recv.at[d, k - 1, h], rs_recv.at[d, k - 1, h])
        return ring_recv[d, k - 1, h].astype(F32)

    def ring_out(d, k, h, incoming=True):
        total = chip_sum(k if d == 0 else 8 - k, h)
        if incoming:
            total = total + ring_in(d, k + 1, h)
        ring_send[d, k - 1, h] = total.astype(BF)
        rs_copies.append(
            remote(
                ring_send.at[d, k - 1, h],
                ring_recv.at[d, k - 1, h],
                rs_send.at[d, k - 1, h],
                rs_recv.at[d, k - 1, h],
                at_z(1 if d == 0 else 7),
            )
        )

    project(4)
    project(3)
    project(5)
    for d in (0, 1):
        ring_out(d, 4, d, incoming=False)
    for d in (0, 1):
        ring_out(d, 3, 1 - d, incoming=False)
    project(2)
    project(6)
    for d in (0, 1):
        ring_out(d, 3, d)
    for d in (0, 1):
        ring_out(d, 2, 1 - d)
    project(1)
    project(7)
    project(0)
    for d in (0, 1):
        ring_out(d, 2, d)
    for d in (0, 1):
        ring_out(d, 1, 1 - d)
    for d in (0, 1):
        ring_out(d, 1, d)

    wait_bytes(shared_sib, sib_recv.at[1])
    shared_send[...] = (shared_part[c].astype(F32) + shared_sib[...].astype(F32)).astype(BF)

    gated = []
    for h in (1, 0):
        rows = pl.ds(h * half_rows, half_rows)
        total = chip_sum(0, h) + ring_in(0, 1, h) + ring_in(1, 1, h)
        gated.append((gate_wide[rows, :] * total).astype(BF))
    gated = jnp.concatenate([gated[1], gated[0]], axis=0)

    for k in FAR_FIRST + (0,):
        xx = (x + k) % 8
        block = picker_t[pl.ds(pl.multiple_of(xx * 128, 128), 128), :]
        expanded[xx] = dot(block, gated).astype(BF)
        if k == 0:
            ret_x[x] = expanded[x]
        else:
            waits_send.append(
                remote(expanded.at[xx], ret_x.at[x], a2a_send.at[2], a2a_recv.at[2], at_x(k))
            )
    for k in FAR_FIRST:
        waits_send.append(
            remote(
                shared_send.at[(z + k) % 8], shared_recv.at[z], tok_send.at[1], tok_recv.at[1], at_z(k)
            )
        )
    shared_recv[z] = shared_send[z]
    selector_t = lax.dot_general(
        one_hot(
            lax.broadcasted_iota(jnp.int32, (128, 128), 0)
            == lax.broadcasted_iota(jnp.int32, (128, 128), 1)
        ),
        selector[...],
        (((1,), (1,)), ((), ())),
        preferred_element_type=F32,
    ).astype(BF)

    wait_bytes(ret_x.at[pl.ds(0, 7)], a2a_recv.at[2])
    for j in range(4):
        added = ret_x[2 * j].astype(F32) + ret_x[2 * j + 1].astype(F32)
        ret_mid[:, j * 16 : (j + 1) * 16, :] = added.astype(BF).reshape(8, 16, 128)
    for k in FAR_FIRST:
        waits_send.append(
            remote(ret_mid.at[(y + k) % 8], ret_y.at[y], a2a_send.at[3], a2a_recv.at[3], at_y(k))
        )
    ret_y[y] = ret_mid[y]

    wait_bytes(shared_recv.at[pl.ds(0, 7)], tok_recv.at[1])
    total = shared_recv[0].astype(F32)
    for n in range(1, 8):
        total = total + shared_recv[n].astype(F32)
    wait_bytes(ret_y.at[pl.ds(0, 7)], a2a_recv.at[3])
    result[...] = (total + dot(selector_t, ret_y[...].reshape(512, 128))).astype(BF)

    for copy in waits_send + tok_copies + ag_copies + sib_copies + rs_copies:
        copy.wait_send()
    tok_sib.wait_send()
    shared_copy.wait_send()


def shards(
    tokens, norm_gain, picks, gates, shared_gate, shared_up, shared_down, expert_in, expert_out
):
    dma = pltpu.SemaphoreType.DMA
    vm = pltpu.VMEM
    return pl.pallas_call(
        layer,
        out_shape=jax.ShapeDtypeStruct((128, 128), BF),
        in_specs=[pl.BlockSpec(memory_space=pl.ANY)] * 9,
        out_specs=pl.BlockSpec(memory_space=pltpu.VMEM),
        scratch_shapes=[
            vm((128, 128), BF),
            vm((16, 128), F32),
            vm((32, 512), jnp.int32),
            vm((32, 512), F32),
            vm((2048, 256), BF),
            vm((128, 2048), BF),
            vm((2048, 256), BF),
            vm((256, 2048), BF),
            vm((512, 128), BF),
            vm((8, 64, 128), BF),
            vm((8, 64, 128), BF),
            vm((8, 8, 16, 128), BF),
            vm((512, 1024), BF),
            vm((1024, 512), BF),
            vm((512, 128), F32),
            vm((2, 8, 128, 128), BF),
            vm((2, 8, 128, 128), BF),
            vm((8, 128, 128), BF),
            vm((8, 128, 128), BF),
            vm((8, 128, 128), BF),
            vm((2, 8, 512, 128), BF),
            vm((512, 256), F32),
            vm((512, 128), F32),
            vm((512, 256), BF),
            vm((8, 2, 512, 128), BF),
            vm((8, 512, 128), BF),
            vm((2, 4, 2, 256, 128), BF),
            vm((2, 4, 2, 256, 128), BF),
            vm((8, 128, 128), BF),
            vm((8, 128, 128), BF),
            vm((8, 64, 128), BF),
            vm((8, 64, 128), BF),
            dma((9,)),
            dma((4,)),
            dma((4,)),
            dma((2,)),
            dma((2,)),
            dma((2,)),
            dma((2,)),
            dma((2, 4, 2)),
            dma((2, 4, 2)),
            dma((8, 2)),
            dma((8, 2)),
            dma((2, 4, 2)),
            dma((2, 4, 2)),
            dma((8,)),
            dma((8,)),
        ],
        compiler_params=pltpu.CompilerParams(
            collective_id=0, has_side_effects=True, vmem_limit_bytes=62 << 20
        ),
        cost_estimate=pl.CostEstimate(
            flops=1_500_000_000, bytes_accessed=4_000_000, transcendentals=200_000
        ),
    )(
        tokens,
        norm_gain.reshape(16, 128),
        picks,
        gates,
        shared_gate,
        shared_up,
        shared_down,
        expert_in,
        expert_out,
    )


def solution(mesh):
    placed = (
        P("expert", "tensor"),
        P(),
        P(),
        P(),
        P(None, "tensor"),
        P(None, "tensor"),
        P("tensor", None),
        P("expert", None, "tensor"),
        P("expert", "tensor", None),
    )
    return jax.shard_map(
        shards, mesh=mesh, in_specs=placed, out_specs=P("expert", "tensor"), check_vma=False
    )
```

time: 211 us -> 82.2 us (0.39)
  waiting for transfers between devices: 107 us -> 0 us
  Pallas kernels: 0 us -> 80.7 us
  starting transfers between devices: 30.1 us -> 0 us
  blocking collectives: 28.8 us -> 0 us
  between operations: 13.6 us -> 0.01 us
  matrix products: 13.2 us -> 0 us
  other arithmetic: 9.87 us -> 0 us
  local copies, waits for them, and re-layouts: 7.15 us -> 1.38 us
    pallas_call x0 -> x1, Pallas kernels: none -> 80.7 us  [shards(): pl.pallas_call(layer, out_shape=jax.ShapeDtypeStruct((128, 128), BF), in_...]
    unnamed x3 -> x0, waiting for transfers between devices: 64.5 us -> none
    all_to_all x2 -> x0, starting transfers between devices: 30 us -> none  [the longest x1 17.2 us: shards(): lax.all_to_all(outgoing, 'expert', split_axis=0, concat_axis=0, tiled=True)]
    all_gather x1 -> x0, blocking collectives: 28.8 us -> none  [shards(): lax.all_gather(tokens, 'tensor', axis=1, tiled=True)]
    all_to_all x2 -> x0, waiting for transfers between devices: 25 us -> none  [the longest x1 12.9 us: shards(): lax.all_to_all(returning.reshape(holders, slot_bound, slice_width), 'expe...]
    all_gather x1 -> x0, waiting for transfers between devices: 17.9 us -> none  [shards(): lax.all_gather(compact, 'tensor', axis=1, tiled=True)]
    dot_general x8 -> x0, matrix products: 13.2 us -> none  [the longest x2 7.08 us: project_rows(): lax.dot_general(weights, hidden, (((0,), (1,)), ((), ())), preferred_elem...]
    unnamed x12 -> x1, local copies, waits for them, and re-layouts: 5.5 us -> 1.38 us
  transfers between devices with their start and end apart: 4 -> 0, of which waited for: 4 -> 0; matrix products, arithmetic and copies ran while one was open for 2% -> 0% of each run, Pallas kernels for 0% -> 0%
where the time goes in v1:
time: 82.2 us; the launch traced here: 82 us
  Pallas kernels  80.7 us (98%)
  local copies, waits for them, and re-layouts  1.38 us (2%)
    pallas_call x1, Pallas kernels, shards(): pl.pallas_call(layer, out_shape=jax.ShapeDtypeStruct((128, 128), BF), in_...  80.7 us

profile of v1, /device:TPU:2, one launch (start us, length us, event | category | flops | bytes accessed | tf_op | source)
XLA Modules:
  0.0 82.0 jit_solution(17370191948405015723)
XLA Ops:
  0.0 80.7 %shard_map.91 = bf16[128,128]{1,0:T(8,128)(2,1)} custom-call(bf16[128,128]{1,0:T(8,128)(2,1)} %tokens_hbm.1, f32[16,128]{1,0:T(8,128)} %bitcast.1, s32[32,512]{1,0:T(8,128)} %picks_hbm.1, f32[32,512]{1,0:T(8,128)} %gates_hbm.1, bf16[2048,128]{1,0:T(8,128)(2,1)} %gate_hbm.1, bf16[2048,128]{1,0:T(8,128)(2,1)} %up_hbm.1, bf16[128,2048]{1,0:T(8,128)(2,1)} %down_hbm.1, ...), custom_call_target="tpu_custom_call" | custom-call | flops 1500000000 | bytes 4000000 | tf_op jit(solution)/shard_map/pallas_call | solution.py:391
  80.7 1.4 %copy.11 = bf16[128,128]{1,0:T(8,128)(2,1)} copy(bf16[128,128]{1,0:T(8,128)(2,1)} %shard_map.91) | data formatting | bytes 65536

commit v2 on v1

--- a/solution.py
+++ b/solution.py
@@ -42,6 +42,8 @@
     z, c = t // 2, t % 2
     other = 1 - c
     half_rows = 256
+    sub_rows = 128
+    subs = ((0, 1, 2, 3), (2, 3, 0, 1))
 
     def at_y(k):
         return (((y + k) % 8) * 8 + x, t)
@@ -146,9 +148,6 @@
     for b in range(8):
         picker[:, b * 128 : (b + 1) * 128] = one_hot(slot_wide == lane + b * 128.0)
 
-    wait_bytes(own_tokens.at[0, pl.ds(0, 7)], tok_recv.at[0])
-    tok_sib = remote(own_tokens.at[c], own_tokens.at[c], sib_send.at[0], sib_recv.at[0], sibling)
-
     def ag_copy(d, k, h):
         src = (z - k + 8) % 8 if d == 0 else (z + k) % 8
         ref = gathered.at[c, src, pl.ds(h * half_rows, half_rows)]
@@ -167,6 +166,9 @@
         for d in (0, 1):
             ag_copies.append(ag_copy(d, 0, h))
         sib_copies.append(ag_sib(z, h, 0))
+
+    wait_bytes(own_tokens.at[0, pl.ds(0, 7)], tok_recv.at[0])
+    tok_sib = remote(own_tokens.at[c], own_tokens.at[c], sib_send.at[0], sib_recv.at[0], sibling)
 
     for b in range(8):
         picker_t[b * 128 : (b + 1) * 128, :] = one_hot(slot == sublane + b * 128.0)
@@ -248,7 +250,8 @@
         previous = k
     last = ag_from(0, 3)
     loads[8].wait()
-    for h in (0, 1):
+
+    def activate(h):
         rows = pl.ds(h * half_rows, half_rows)
         sib_wait(last, h, 7)
         absorb(h, [(c, last), (other, last)])
@@ -258,80 +261,90 @@
 
     rs_copies = []
 
-    def project(k):
+    def project(k, h):
         column = pl.multiple_of((z + k) % 8 * 256, 256)
-        weight = w_out[:, pl.ds(column, 256)]
-        for h in (0, 1):
-            rows = pl.ds(h * half_rows, half_rows)
-            term = dot(activation[rows, :], weight).astype(BF)
-            partial[k, 0, rows] = term[:, :128]
-            partial[k, 1, rows] = term[:, 128:]
+        rows = pl.ds(h * half_rows, half_rows)
+        term = dot(activation[rows, :], w_out[:, pl.ds(column, 256)]).astype(BF)
+        partial[k, 0, rows] = term[:, :128]
+        partial[k, 1, rows] = term[:, 128:]
         rs_copies.append(
             remote(
-                partial.at[k, other], partial_sib.at[k], rssib_send.at[k], rssib_recv.at[k], sibling
+                partial.at[k, other, rows],
+                partial_sib.at[k, rows],
+                rssib_send.at[k, h],
+                rssib_recv.at[k, h],
+                sibling,
             )
         )
 
     arrived = set()
 
-    def chip_sum(k, h):
-        if k not in arrived:
-            arrived.add(k)
-            wait_bytes(partial_sib.at[k], rssib_recv.at[k])
-        rows = pl.ds(h * half_rows, half_rows)
+    def chip_sum(k, s):
+        h = s // 2
+        if (k, h) not in arrived:
+            arrived.add((k, h))
+            wait_bytes(partial_sib.at[k, pl.ds(h * half_rows, half_rows)], rssib_recv.at[k, h])
+        rows = pl.ds(s * sub_rows, sub_rows)
         return partial[k, c, rows].astype(F32) + partial_sib[k, rows].astype(F32)
 
-    def ring_in(d, k, h):
-        wait_bytes(ring_recv.at[d, k - 1, h], rs_recv.at[d, k - 1, h])
-        return ring_recv[d, k - 1, h].astype(F32)
-
-    def ring_out(d, k, h, incoming=True):
-        total = chip_sum(k if d == 0 else 8 - k, h)
+    def ring_in(d, k, s):
+        wait_bytes(ring_recv.at[d, k - 1, s], rs_recv.at[d, k - 1, s])
+        return ring_recv[d, k - 1, s].astype(F32)
+
+    def ring_out(d, k, s, incoming=True):
+        total = chip_sum(k if d == 0 else 8 - k, s)
         if incoming:
-            total = total + ring_in(d, k + 1, h)
-        ring_send[d, k - 1, h] = total.astype(BF)
+            total = total + ring_in(d, k + 1, s)
+        ring_send[d, k - 1, s] = total.astype(BF)
         rs_copies.append(
             remote(
-                ring_send.at[d, k - 1, h],
-                ring_recv.at[d, k - 1, h],
-                rs_send.at[d, k - 1, h],
-                rs_recv.at[d, k - 1, h],
+                ring_send.at[d, k - 1, s],
+                ring_recv.at[d, k - 1, s],
+                rs_send.at[d, k - 1, s],
+                rs_recv.at[d, k - 1, s],
                 at_z(1 if d == 0 else 7),
             )
         )
 
-    project(4)
-    project(3)
-    project(5)
-    for d in (0, 1):
-        ring_out(d, 4, d, incoming=False)
-    for d in (0, 1):
-        ring_out(d, 3, 1 - d, incoming=False)
-    project(2)
-    project(6)
-    for d in (0, 1):
-        ring_out(d, 3, d)
-    for d in (0, 1):
-        ring_out(d, 2, 1 - d)
-    project(1)
-    project(7)
-    project(0)
-    for d in (0, 1):
-        ring_out(d, 2, d)
-    for d in (0, 1):
-        ring_out(d, 1, 1 - d)
-    for d in (0, 1):
-        ring_out(d, 1, d)
+    def ring_step(k, part, incoming=True):
+        for i in (2 * part, 2 * part + 1):
+            for d in (0, 1):
+                ring_out(d, k, subs[d][i], incoming)
+
+    activate(0)
+    project(4, 0)
+    project(5, 0)
+    activate(1)
+    project(4, 1)
+    project(3, 1)
+    ring_step(4, 0, incoming=False)
+    project(3, 0)
+    ring_step(3, 1, incoming=False)
+    project(5, 1)
+    project(2, 1)
+    project(6, 0)
+    ring_step(3, 0)
+    project(2, 0)
+    project(6, 1)
+    ring_step(2, 1)
+    project(1, 1)
+    project(7, 0)
+    ring_step(2, 0)
+    project(1, 0)
+    project(7, 1)
+    ring_step(1, 1)
+    project(0, 0)
+    project(0, 1)
+    ring_step(1, 0)
 
     wait_bytes(shared_sib, sib_recv.at[1])
     shared_send[...] = (shared_part[c].astype(F32) + shared_sib[...].astype(F32)).astype(BF)
 
-    gated = []
-    for h in (1, 0):
-        rows = pl.ds(h * half_rows, half_rows)
-        total = chip_sum(0, h) + ring_in(0, 1, h) + ring_in(1, 1, h)
-        gated.append((gate_wide[rows, :] * total).astype(BF))
-    gated = jnp.concatenate([gated[1], gated[0]], axis=0)
+    gated = [None] * 4
+    for s in (2, 3, 0, 1):
+        total = chip_sum(0, s) + ring_in(0, 1, s) + ring_in(1, 1, s)
+        gated[s] = (gate_wide[s * sub_rows : (s + 1) * sub_rows, :] * total).astype(BF)
+    gated = jnp.concatenate(gated, axis=0)
 
     for k in FAR_FIRST + (0,):
         xx = (x + k) % 8
@@ -360,6 +373,14 @@
         preferred_element_type=F32,
     ).astype(BF)
 
+    wait_bytes(mid.at[pl.ds(0, 7)], a2a_send.at[0])
+    wait_bytes(slots.at[pl.ds(0, 7)], a2a_send.at[1])
+    wait_bytes(own_tokens.at[0, pl.ds(0, 7)], tok_send.at[0])
+    for copy in ag_copies + sib_copies + rs_copies:
+        copy.wait_send()
+    tok_sib.wait_send()
+    shared_copy.wait_send()
+
     wait_bytes(ret_x.at[pl.ds(0, 7)], a2a_recv.at[2])
     for j in range(4):
         added = ret_x[2 * j].astype(F32) + ret_x[2 * j + 1].astype(F32)
@@ -377,10 +398,9 @@
     wait_bytes(ret_y.at[pl.ds(0, 7)], a2a_recv.at[3])
     result[...] = (total + dot(selector_t, ret_y[...].reshape(512, 128))).astype(BF)
 
-    for copy in waits_send + tok_copies + ag_copies + sib_copies + rs_copies:
-        copy.wait_send()
-    tok_sib.wait_send()
-    shared_copy.wait_send()
+    wait_bytes(ret_x.at[pl.ds(0, 7)], a2a_send.at[2])
+    wait_bytes(ret_y.at[pl.ds(0, 7)], a2a_send.at[3])
+    wait_bytes(shared_recv.at[pl.ds(0, 7)], tok_send.at[1])
 
 
 def shards(
@@ -420,8 +440,8 @@
             vm((512, 256), BF),
             vm((8, 2, 512, 128), BF),
             vm((8, 512, 128), BF),
-            vm((2, 4, 2, 256, 128), BF),
-            vm((2, 4, 2, 256, 128), BF),
+            vm((2, 4, 4, 128, 128), BF),
+            vm((2, 4, 4, 128, 128), BF),
             vm((8, 128, 128), BF),
             vm((8, 128, 128), BF),
             vm((8, 64, 128), BF),
@@ -437,10 +457,10 @@
             dma((2, 4, 2)),
             dma((8, 2)),
             dma((8, 2)),
-            dma((2, 4, 2)),
-            dma((2, 4, 2)),
-            dma((8,)),
-            dma((8,)),
+            dma((2, 4, 4)),
+            dma((2, 4, 4)),
+            dma((8, 2)),
+            dma((8, 2)),
         ],
         compiler_params=pltpu.CompilerParams(
             collective_id=0, has_side_effects=True, vmem_limit_bytes=62 << 20

time: 82.2 us -> 81.5 us (level)
  no operation moved by 1% of the time
where the time goes in v2:
time: 81.5 us; the launch traced here: 81.3 us
  Pallas kernels  79.9 us (98%)
  local copies, waits for them, and re-layouts  1.38 us (2%)
    pallas_call x1, Pallas kernels, shards(): pl.pallas_call(layer, out_shape=jax.ShapeDtypeStruct((128, 128), BF), in_...  79.9 us

profile of v2, /device:TPU:2, one launch (start us, length us, event | category | flops | bytes accessed | tf_op | source)
XLA Modules:
  0.0 81.3 jit_solution(15953271648310967076)
XLA Ops:
  0.0 79.9 %shard_map.91 = bf16[128,128]{1,0:T(8,128)(2,1)} custom-call(bf16[128,128]{1,0:T(8,128)(2,1)} %tokens_hbm.1, f32[16,128]{1,0:T(8,128)} %bitcast.1, s32[32,512]{1,0:T(8,128)} %picks_hbm.1, f32[32,512]{1,0:T(8,128)} %gates_hbm.1, bf16[2048,128]{1,0:T(8,128)(2,1)} %gate_hbm.1, bf16[2048,128]{1,0:T(8,128)(2,1)} %up_hbm.1, bf16[128,2048]{1,0:T(8,128)(2,1)} %down_hbm.1, ...), custom_call_target="tpu_custom_call" | custom-call | flops 1500000000 | bytes 4000000 | tf_op jit(solution)/shard_map/pallas_call | solution.py:411
  79.9 1.4 %copy.11 = bf16[128,128]{1,0:T(8,128)(2,1)} copy(bf16[128,128]{1,0:T(8,128)(2,1)} %shard_map.91) | data formatting | bytes 65536
